TPU v7x, 32 devices: a whole 2x2x4 slice. The times are simulated.
32 devices in a mesh: row: 4 (over y, core), col: 8 (over z, x).
Axes of the slice: x: 2, y: 2, z: 4, core: 2. Of those that a mesh axis runs over, the one named last changes fastest.
Arguments:
- tokens: bfloat16 [128, 8192], P('col', 'row'), may hold values from -120 to 120
- source: int32 [128], replicated, may hold values from 0 to 127, each once
- gain: float32 [8192], P('row'), may hold values from 0.5 to 1.5
- gate_weight: bfloat16 [8192, 29568], P('row', 'col'), may hold values from -0.0625 to 0.0625
- up_weight: bfloat16 [8192, 29568], P('row', 'col'), may hold values from -0.0625 to 0.0625
- down_weight: bfloat16 [29568, 8192], P('col', 'row'), may hold values from -0.03125 to 0.03125
Outputs:
- mixed: bfloat16 [128, 8192], P('col', 'row')
All inputs are finite; a program needn't handle non-finite values.
Results may differ from a plain program's by a relative error of at most 0.0064.
Values may be sent and summed in bfloat16 or wider, within the bound.
A program may use at most 128 MiB of HBM per device.

v0:
```python
import jax
import jax.numpy as jnp
from jax import lax
from jax.sharding import PartitionSpec as P

D = 8192


def activate(gate_sum, up_sum, square_sum):
    scale = lax.rsqrt(square_sum / D + 1e-06)
    return (jax.nn.silu(scale * gate_sum) * (scale * up_sum)).astype(jnp.bfloat16)


def on_device(tokens, source, gain, gate_weight, up_weight, down_weight):
    gathered = lax.all_gather(tokens, "col", axis=0, tiled=True)
    merged = jnp.take(gathered, source, axis=0).astype(jnp.float32)
    squares = jnp.sum(merged * merged, axis=1, keepdims=True)
    square_all = lax.psum(squares, "row")
    weighted = (merged * gain).astype(jnp.bfloat16)
    gate_part = jnp.dot(weighted, gate_weight, preferred_element_type=jnp.float32)
    up_part = jnp.dot(weighted, up_weight, preferred_element_type=jnp.float32)
    gate_sum, up_sum = (
        lax.psum_scatter(gate_part, "row", scatter_dimension=0, tiled=True),
        lax.psum_scatter(up_part, "row", scatter_dimension=0, tiled=True),
    )
    share = gate_sum.shape[0]
    square_sum = lax.dynamic_slice_in_dim(square_all, lax.axis_index("row") * share, share, 0)
    hidden_all = lax.all_gather(activate(gate_sum, up_sum, square_sum), "row", axis=0, tiled=True)
    mixed = lax.psum_scatter(
        jnp.dot(hidden_all, down_weight, preferred_element_type=jnp.float32),
        "col",
        scatter_dimension=0,
        tiled=True,
    )
    return mixed.astype(jnp.bfloat16)


def solution(mesh):
    return jax.shard_map(
        on_device,
        mesh=mesh,
        in_specs=(
            P("col", "row"),
            P(),
            P("row"),
            P("row", "col"),
            P("row", "col"),
            P("col", "row"),
        ),
        out_specs=P("col", "row"),
        check_vma=False,
    )
```

profile of v0, /device:TPU:0, one launch (start us, length us, event | category | flops | bytes accessed | tf_op | source)
XLA Modules:
  0.0 210.0 jit_solution(17975841860871017839)
XLA Ops:
  6.5 0.0 copy-start
  6.5 0.0 reduce-scatter.4.cloned.1.call-start
  6.5 0.7 compare_and_fusion
  7.2 0.7 compare_select_fusion
  7.9 33.2 %all_gather.6 = bf16[128,2048]{1,0:T(8,128)(2,1)S(1)} all-gather(bf16[16,2048]{1,0:T(8,128)(2,1)} %param.6), channel_id=1, replica_groups=mesh['row'=4,'col'=8] {'col'}, dimensions={0}, use_global_device_ids=true | all-gather | bytes 589824 | tf_op jit(solution)/shard_map/all_gather | solution.py:15
  41.1 0.9 gather_fusion
  42.0 11.8 %fusion.4 = f32[128,3696]{1,0:T(8,128)} fusion(bf16[2048,3696]{0,1:T(8,128)(2,1)} %param.9, f32[2048]{0:T(1024)} %param.8, bf16[128,2048]{1,0:T(8,128)(2,1)S(1)} %gather_fusion, pred[128]{0:T(512)(128)(4,1)S(1)} %compare_and_fusion), kind=kOutput, calls=%fused_computation.8 | convolution fusion | flops 1938817024 | bytes 17563776 | tf_op jit(solution)/shard_map/dot_general | solution.py:20
  53.8 0.0 reduce-scatter.4.cloned.1.call-update
  53.8 0.0 reduce-scatter.6.cloned.1.call-start
  53.9 0.0 copy-done
  53.9 11.7 %fusion.2 = f32[128,3696]{1,0:T(8,128)} fusion(bf16[2048,3696]{0,1:T(8,128)(2,1)} %param.10, f32[2048]{0:T(1024)S(1)} %copy-done, bf16[128,2048]{1,0:T(8,128)(2,1)S(1)} %gather_fusion, pred[128]{0:T(512)(128)(4,1)S(1)} %compare_and_fusion), kind=kOutput, calls=%fused_computation.7 | convolution fusion | flops 1938817024 | bytes 17563776 | tf_op jit(solution)/shard_map/dot_general | solution.py:21
  65.6 0.0 reduce-scatter.6.cloned.1.call-update
  65.6 0.0 reduce-scatter.8.cloned.1.call-start
  65.7 0.3 fusion
  66.0 5.7 %psum.7 = f32[128,1]{0,1:T(1,128)S(1)} all-reduce(f32[128,1]{0,1:T(1,128)S(1)} %bitcast.7), channel_id=1, replica_groups=mesh['row'=4,'col'=8] {'row'}, use_global_device_ids=true, to_apply=%region_1.2 | all-reduce | flops 128 | bytes 1024 | tf_op jit(solution)/shard_map/psum | solution.py:18
  71.7 0.1 rsqrt_bitcast_fusion
  71.7 13.6 %reduce-scatter.4.cloned.1.call-done = f32[32,3696]{1,0:T(8,128)} async-done(((f32[128,3696]{1,0:T(8,128)}), f32[32,3696]{1,0:T(8,128)}) %reduce-scatter.4.cloned.1.call-update) | async-done | bytes 473104 | tf_op jit(solution)/shard_map/reduce_scatter | solution.py:23
  85.3 33.1 %reduce-scatter.6.cloned.1.call-done = f32[32,3696]{1,0:T(8,128)} async-done(((f32[128,3696]{1,0:T(8,128)}), f32[32,3696]{1,0:T(8,128)}) %reduce-scatter.6.cloned.1.call-update) | async-done | bytes 473104 | tf_op jit(solution)/shard_map/reduce_scatter | solution.py:24
  118.4 1.4 multiply_convert_fusion
  119.8 9.1 %all_gather.7 = bf16[128,3696]{1,0:T(8,128)(2,1)S(1)} all-gather(bf16[32,3696]{1,0:T(8,128)(2,1)S(1)} %multiply_convert_fusion), channel_id=1, replica_groups=mesh['row'=4,'col'=8] {'row'}, dimensions={0}, use_global_device_ids=true | all-gather | bytes 1182720 | tf_op jit(solution)/shard_map/all_gather | solution.py:28
  128.9 8.7 %fusion.6 = f32[128,2048]{1,0:T(8,128)} fusion(bf16[128,3696]{1,0:T(8,128)(2,1)S(1)} %all_gather.7, bf16[3696,2048]{1,0:T(8,128)(2,1)} %param.11), kind=kOutput, calls=%fused_computation.13 | convolution fusion | flops 1937768448 | bytes 17133568 | tf_op jit(solution)/shard_map/dot_general | solution.py:30
  137.6 0.0 reduce-scatter.8.cloned.1.call-update
  137.6 64.4 %reduce-scatter.8.cloned.1.call-done = f32[16,2048]{1,0:T(8,128)} async-done(((f32[128,2048]{1,0:T(8,128)}), f32[16,2048]{1,0:T(8,128)}) %reduce-scatter.8.cloned.1.call-update) | async-done | bytes 131088 | tf_op jit(solution)/shard_map/reduce_scatter | solution.py:29
  202.0 1.5 convert_element_type.15
  (1 shorter events, 0.0 us)
Async XLA Ops:
  6.5 47.4 %copy-start = (f32[2048]{0:T(1024)S(1)}, f32[2048]{0:T(1024)}, u32[]{:S(2)}) copy-start(f32[2048]{0:T(1024)} %param.8) | copy-start | bytes 24580
  6.5 78.8 %reduce-scatter.4.cloned.1.call-start = ((), (), s32[]{:S(2)}) async-start(), calls=%async_computation.3 | async-start | bytes 2375680 | tf_op jit(solution)/shard_map/reduce_scatter | solution.py:23
  53.8 64.6 %reduce-scatter.6.cloned.1.call-start = ((), (), s32[]{:S(2)}) async-start(), calls=%async_computation.4 | async-start | bytes 2375680 | tf_op jit(solution)/shard_map/reduce_scatter | solution.py:24
  65.6 136.3 %reduce-scatter.8.cloned.1.call-start = ((), (), s32[]{:S(2)}) async-start(), calls=%async_computation.5 | async-start | bytes 1179648 | tf_op jit(solution)/shard_map/reduce_scatter | solution.py:29
Sparse Core Ops, SparseCore 0:
  54.0 31.3 reduce-scatter.3
  88.1 30.3 reduce-scatter.5
  137.7 64.1 reduce-scatter.7
where the time goes:
time: 210 us
  waiting for transfers between devices  111 us (53%)
  blocking collectives  48 us (23%)
  matrix products  32.2 us (15%)
  between operations  13.1 us (6%)
  other arithmetic  4.62 us (2%)
    reduce_scatter x1, waiting for transfers between devices, on_device(): lax.psum_scatter(jnp.dot(hidden_all, down_weight, preferred_element_type=...  64.4 us
    all_gather x1, blocking collectives, on_device(): gathered = lax.all_gather(tokens, 'col', axis=0, tiled=True)  33.2 us
    reduce_scatter x1, waiting for transfers between devices, on_device(): lax.psum_scatter(up_part, 'row', scatter_dimension=0, tiled=True)  33.1 us
    reduce_scatter x1, waiting for transfers between devices, on_device(): lax.psum_scatter(gate_part, 'row', scatter_dimension=0, tiled=True)  13.6 us
    dot_general x1, matrix products, on_device(): jnp.dot(weighted, gate_weight, preferred_element_type=jnp.float32)  11.8 us
    dot_general x1, matrix products, on_device(): up_part = jnp.dot(weighted, up_weight, preferred_element_type=jnp.float32)  11.7 us
    all_gather x1, blocking collectives, on_device(): lax.all_gather(activate(gate_sum, up_sum, square_sum), 'row', axis=0, til...  9.11 us
    dot_general x1, matrix products, on_device(): jnp.dot(hidden_all, down_weight, preferred_element_type=jnp.float32)  8.7 us
  transfers between devices with their start and end apart: 3, of which 3 were waited for; matrix products, arithmetic and copies ran while one was open for 6% of the time, Pallas kernels for 0%

commit v1 on v0

v1 whole, which is shorter than its diff:
```python
import functools

import jax
import jax.numpy as jnp
from jax import lax
from jax.experimental import pallas as pl
from jax.experimental.pallas import tpu as pltpu
from jax.sharding import PartitionSpec as P

F32 = jnp.float32
BF16 = jnp.bfloat16
TILE = 256
CHUNK = 512
PIECES = 4


def chunks_of(width):
    count = max(1, -(-(width - TILE) // CHUNK))
    starts = [i * CHUNK for i in range(count)]
    ends = starts[1:] + [width]
    return [(a, b - a) for a, b in zip(starts, ends)]


def lanes(width):
    return -(-width // 128) * 128


def kernel(R, C, chunks, tok_ref, src_ref, gain_ref, wg_hbm, wu_hbm, wd_hbm, out_ref,
           wg, wu, wd, G, wt, sq_out, sq_in, part, sendA, recvA, own, sendB, recvB, H,
           acc, sendX, recvX, sendZ, recvZ,
           wg_sem, wu_sem, wd_sem, agz_s, agz_r, agx_s, agx_r, sq_s, sq_r,
           a_s, a_r, b_s, b_r, hy_s, hy_r, hs_s, hs_r, x_s, x_r, z_s, z_r):
    Y, Z = R // 2, C // 2
    T = wt.shape[0]
    Dl = wt.shape[1]
    S = T // R
    Tc = T // C
    n = len(chunks)
    r = lax.axis_index("row")
    c = lax.axis_index("col")
    y, k = r // 2, lax.rem(r, 2)
    z, x = c // 2, lax.rem(c, 2)
    sib = {"row": y * 2 + (1 - k)}
    mate = {"col": z * 2 + (1 - x)}

    def ynext(d):
        return lax.rem(y + d, Y)

    def znext(d):
        return lax.rem(z + d, Z)

    def remote(src, dst, s, rv, dev):
        return pltpu.make_async_remote_copy(
            src_ref=src, dst_ref=dst, send_sem=s, recv_sem=rv, device_id=dev,
            device_id_type=pl.DeviceIdType.MESH)

    loads = {"g": [], "u": [], "d": []}
    parts = wg_sem.shape[0]
    step = Dl // parts
    for name, hbm, vm, sem in (("g", wg_hbm, wg, wg_sem), ("u", wu_hbm, wu, wu_sem)):
        for i in range(parts):
            cp = pltpu.make_async_copy(hbm.at[pl.ds(i * step, step)], vm.at[pl.ds(i * step, step)], sem.at[i])
            cp.start()
            loads[name].append(cp)
    for i, (c0, w) in enumerate(chunks):
        cp = pltpu.make_async_copy(wd_hbm.at[pl.ds(c0, w)], wd.at[pl.ds(c0, w)], wd_sem.at[i])
        cp.start()
        loads["d"].append(cp)

    barrier = pltpu.get_barrier_semaphore()
    for d in range(1, R):
        pl.semaphore_signal(barrier, inc=1, device_id={"row": lax.rem(r + d, R)},
                            device_id_type=pl.DeviceIdType.MESH)
    for d in range(1, Z):
        pl.semaphore_signal(barrier, inc=1, device_id={"col": znext(d) * 2 + x},
                            device_id_type=pl.DeviceIdType.MESH)
    pl.semaphore_signal(barrier, inc=1, device_id=mate, device_id_type=pl.DeviceIdType.MESH)
    G[c] = tok_ref[...]
    pl.semaphore_wait(barrier, R - 1 + Z - 1 + 1)

    sent = []

    def ag_forward(d):
        block = lax.rem(z + Z - d, Z) * 2 + x
        cp = remote(G.at[block], G.at[block], agx_s.at[d], agx_r.at[d], mate)
        cp.start()
        sent.append(cp)
        return cp

    along = []
    for d in range(1, Z):
        cp = remote(G.at[c], G.at[c], agz_s.at[d - 1], agz_r.at[d - 1], {"col": znext(d) * 2 + x})
        cp.start()
        along.append(cp)
        sent.append(cp)
    across = [ag_forward(0)]
    order = sorted(range(1, Z), key=lambda d: min(d, Z - d))
    for d in order:
        along[d - 1].wait_recv()
        across.append(ag_forward(d))
    for cp in across:
        cp.wait_recv()

    pick = (src_ref[...] == lax.broadcasted_iota(jnp.int32, (T, T), 1)).astype(BF16)
    fw = min(512, Dl)
    total = jnp.zeros((T, 1), F32)
    for f in range(Dl // fw):
        cols = slice(f * fw, (f + 1) * fw)
        m = jnp.dot(pick, G[:, :, cols].reshape(T, fw), preferred_element_type=F32)
        total = total + jnp.sum(m * m, axis=1, keepdims=True)
        wt[:, cols] = (m * gain_ref[:, cols]).astype(BF16)
    sq_out[...] = jnp.broadcast_to(total, (T, 128)).reshape(R, S, 128)
    squares = []
    for d in range(1, R):
        to = lax.rem(r + d, R)
        cp = remote(sq_out.at[to], sq_in.at[d - 1], sq_s.at[d - 1], sq_r.at[d - 1], {"row": to})
        cp.start()
        squares.append(cp)
        sent.append(cp)

    copies = {}

    def product(u):
        j, s = u // 2, u % 2
        c0, w = chunks[j]
        W = wu if s else wg
        if u < 2:
            for cp in loads["u" if s else "g"]:
                cp.wait()
        full = w // TILE

        def body(t, _):
            off = pl.multiple_of(t * TILE, TILE)
            v = jnp.dot(wt[...], W[:, pl.ds(pl.multiple_of(c0 + off, TILE), TILE)], preferred_element_type=F32)
            part[s, :, :, pl.ds(off, TILE)] = v.reshape(R, S, TILE)
            return 0

        lax.fori_loop(0, full, body, 0)
        rest = w - full * TILE
        if rest:
            v = jnp.dot(wt[...], W[:, c0 + full * TILE:c0 + w], preferred_element_type=F32)
            part[s, :, :, full * TILE:w] = v.reshape(R, S, rest)
        wp = lanes(w)
        for yy in range(Y):
            sendA[j, s, yy, :, :w] = part[s, yy * 2 + (1 - k), :, :w].astype(BF16)
        cp = remote(sendA.at[j, s, :, :, pl.ds(0, wp)], recvA.at[j, s, :, :, pl.ds(0, wp)],
                    a_s.at[j, s], a_r.at[j, s], sib)
        cp.start()
        copies["a", u] = cp
        sent.append(cp)

    def pair_sum(u):
        j, s = u // 2, u % 2
        w = chunks[j][1]
        wp = lanes(w)
        copies["a", u].wait_recv()
        for d in range(1, Y):
            to = ynext(d)
            sendB[j, s, d - 1, :, :w] = (
                part[s, to * 2 + k, :, :w] + recvA[j, s, to, :, :w].astype(F32)).astype(BF16)
            cp = remote(sendB.at[j, s, d - 1, :, pl.ds(0, wp)], recvB.at[j, s, d - 1, :, pl.ds(0, wp)],
                        b_s.at[j, s, d - 1], b_r.at[j, s, d - 1], {"row": to * 2 + k})
            cp.start()
            copies["b", u, d] = cp
            sent.append(cp)
        own[j, s, :, :w] = part[s, r, :, :w] + recvA[j, s, y, :, :w].astype(F32)

    def hidden(j):
        w = chunks[j][1]
        wp = lanes(w)
        if j == 0:
            for cp in squares:
                cp.wait_recv()
        sq = sq_out[r]
        for d in range(1, R):
            sq = sq + sq_in[d - 1]
        scale = lax.rsqrt(sq[:, :1] / (Dl * R) + 1e-6)
        sums = []
        for s in range(2):
            v = own[j, s, :, :w]
            for d in range(1, Y):
                copies["b", 2 * j + s, d].wait_recv()
                v = v + recvB[j, s, d - 1, :, :w].astype(F32)
            sums.append(scale * v)
        gate, up = sums
        H[j, r, :, :w] = (gate / (1.0 + jnp.exp(-gate)) * up).astype(BF16)
        for d in range(1, Y):
            view = H.at[j, r, :, pl.ds(0, wp)]
            cp = remote(view, view, hy_s.at[j, d - 1], hy_r.at[j, d - 1], {"row": ynext(d) * 2 + k})
            cp.start()
            copies["hy", j, d] = cp
            sent.append(cp)
        to_sibling(j, 0)

    def to_sibling(j, d):
        wp = lanes(chunks[j][1])
        view = H.at[j, lax.rem(y + Y - d, Y) * 2 + k, :, pl.ds(0, wp)]
        cp = remote(view, view, hs_s.at[j, d], hs_r.at[j, d], sib)
        cp.start()
        copies["hs", j, d] = cp
        sent.append(cp)

    def forward(j):
        for d in range(1, Y):
            copies["hy", j, d].wait_recv()
            to_sibling(j, d)

    def down_cols(j, first, count):
        c0, w = chunks[j]
        tile = min(TILE, Dl // PIECES)

        def body(t, _):
            cols = pl.ds(pl.multiple_of(first + t * tile, 128), tile)
            v = jnp.dot(H[j, :, :, :w].reshape(T, w), wd[c0:c0 + w, cols], preferred_element_type=F32)
            v = v.reshape(C, Tc, tile)
            acc[:, :, cols] = v if j == 0 else acc[:, :, cols] + v
            return 0

        lax.fori_loop(0, count // tile, body, 0)

    def down_ready(j):
        for d in range(Y):
            copies["hs", j, d].wait_recv()
        loads["d"][j].wait()

    width = Dl // PIECES

    def send_across(p):
        cols = slice(p * width, (p + 1) * width)
        for zz in range(Z):
            sendX[p, zz] = acc[zz * 2 + (1 - x), :, cols].astype(BF16)
        cp = remote(sendX.at[p], recvX.at[p], x_s.at[p], x_r.at[p], mate)
        cp.start()
        copies["x", p] = cp
        sent.append(cp)

    def send_along(p):
        cols = slice(p * width, (p + 1) * width)
        copies["x", p].wait_recv()
        for d in sorted(range(1, Z), key=lambda d: -min(d, Z - d)):
            to = znext(d)
            sendZ[p, d - 1] = (acc[to * 2 + x, :, cols] + recvX[p, to].astype(F32)).astype(BF16)
            cp = remote(sendZ.at[p, d - 1], recvZ.at[p, d - 1], z_s.at[p, d - 1], z_r.at[p, d - 1],
                        {"col": to * 2 + x})
            cp.start()
            copies["z", p, d] = cp
            sent.append(cp)

    def finish(p):
        cols = slice(p * width, (p + 1) * width)
        v = acc[c, :, cols] + recvX[p, z].astype(F32)
        for d in range(1, Z):
            copies["z", p, d].wait_recv()
            v = v + recvZ[p, d - 1].astype(F32)
        out_ref[:, cols] = v.astype(BF16)

    for i in range(n + 4):
        for s in range(2):
            u = 2 * i + s
            if u < 2 * n:
                product(u)
            if 0 <= u - 1 < 2 * n:
                pair_sum(u - 1)
        if 0 <= i - 2 < n:
            hidden(i - 2)
        if 0 <= i - 3 < n:
            forward(i - 3)
        if 0 <= i - 4 < n - 1:
            down_ready(i - 4)
            down_cols(i - 4, 0, Dl)
    down_ready(n - 1)
    for p in range(PIECES):
        down_cols(n - 1, p * width, width)
        send_across(p)
        if p:
            send_along(p - 1)
    send_along(PIECES - 1)
    for p in range(PIECES):
        finish(p)
    for cp in sent:
        cp.wait_send()


def on_device(R, C, tokens, source, gain, gate_weight, up_weight, down_weight):
    Tc, Dl = tokens.shape
    T = Tc * C
    S = T // R
    Y, Z = R // 2, C // 2
    FL = gate_weight.shape[1]
    chunks = chunks_of(FL)
    n = len(chunks)
    wmax = max(lanes(w) for _, w in chunks)
    width = Dl // PIECES
    dma = pltpu.SemaphoreType.DMA
    vm = pltpu.VMEM
    loads = 4
    scratch = [
        vm((Dl, FL), BF16), vm((Dl, FL), BF16), vm((FL, Dl), BF16),
        vm((C, Tc, Dl), BF16), vm((T, Dl), BF16),
        vm((R, S, 128), F32), vm((R - 1, S, 128), F32),
        vm((2, R, S, wmax), F32),
        vm((n, 2, Y, S, wmax), BF16), vm((n, 2, Y, S, wmax), BF16),
        vm((n, 2, S, wmax), F32),
        vm((n, 2, Y - 1, S, wmax), BF16), vm((n, 2, Y - 1, S, wmax), BF16),
        vm((n, R, S, wmax), BF16),
        vm((C, Tc, Dl), F32),
        vm((PIECES, Z, Tc, width), BF16), vm((PIECES, Z, Tc, width), BF16),
        vm((PIECES, Z - 1, Tc, width), BF16), vm((PIECES, Z - 1, Tc, width), BF16),
        dma((loads,)), dma((loads,)), dma((n,)),
        dma((Z - 1,)), dma((Z - 1,)), dma((Z,)), dma((Z,)), dma((R - 1,)), dma((R - 1,)),
        dma((n, 2)), dma((n, 2)), dma((n, 2, Y - 1)), dma((n, 2, Y - 1)),
        dma((n, Y - 1)), dma((n, Y - 1)), dma((n, Y)), dma((n, Y)),
        dma((PIECES,)), dma((PIECES,)), dma((PIECES, Z - 1)), dma((PIECES, Z - 1)),
    ]
    vspec = pl.BlockSpec(memory_space=pltpu.VMEM)
    hspec = pl.BlockSpec(memory_space=pl.ANY)
    return pl.pallas_call(
        functools.partial(kernel, R, C, chunks),
        out_shape=jax.ShapeDtypeStruct((Tc, Dl), BF16),
        in_specs=[vspec, vspec, vspec, hspec, hspec, hspec],
        out_specs=vspec,
        scratch_shapes=scratch,
        compiler_params=pltpu.CompilerParams(
            collective_id=0, has_side_effects=True, vmem_limit_bytes=62 * 1024 * 1024),
        cost_estimate=pl.CostEstimate(
            flops=6 * T * Dl * FL, bytes_accessed=6 * Dl * FL, transcendentals=S * FL),
        name="feed_forward",
    )(tokens, source.reshape(T, 1), gain.reshape(1, Dl), gate_weight, up_weight, down_weight)


def solution(mesh):
    return jax.shard_map(
        functools.partial(on_device, mesh.shape["row"], mesh.shape["col"]),
        mesh=mesh,
        in_specs=(
            P("col", "row"),
            P(),
            P("row"),
            P("row", "col"),
            P("row", "col"),
            P("col", "row"),
        ),
        out_specs=P("col", "row"),
        check_vma=False,
    )
```

time: 210 us -> 102 us (0.49)
  waiting for transfers between devices: 111 us -> 0 us
  Pallas kernels: 0 us -> 60.3 us
  blocking collectives: 48 us -> 0 us
  local copies, waits for them, and re-layouts: 0.94 us -> 41 us
  matrix products: 32.2 us -> 0 us
  between operations: 13.1 us -> 0.01 us
  other arithmetic: 4.62 us -> 0 us
    reduce_scatter x3 -> x0, waiting for transfers between devices: 111 us -> none  [the longest x1 64.4 us: on_device(): lax.psum_scatter(jnp.dot(hidden_all, down_weight, preferred_element_type=...]
    pallas_call x0 -> x1, Pallas kernels: none -> 60.3 us  [on_device(): pl.pallas_call(functools.partial(kernel, R, C, chunks), out_shape=jax.Sha...]
    all_gather x2 -> x0, blocking collectives: 42.3 us -> none  [the longest x1 33.2 us: on_device(): gathered = lax.all_gather(tokens, 'col', axis=0, tiled=True)]
    unnamed x2 -> x3, local copies, waits for them, and re-layouts: 0.01 us -> 39.7 us
    dot_general x3 -> x0, matrix products: 32.2 us -> none  [the longest x1 11.8 us: on_device(): jnp.dot(weighted, gate_weight, preferred_element_type=jnp.float32)]
    psum x1 -> x0, blocking collectives: 5.66 us -> none  [on_device(): square_all = lax.psum(squares, 'row')]
    convert_element_type x2 -> x0, other arithmetic: 2.92 us -> none  [the longest x1 1.54 us: on_device(): return mixed.astype(jnp.bfloat16)]
  transfers between devices with their start and end apart: 3 -> 0, of which waited for: 3 -> 0; matrix products, arithmetic and copies ran while one was open for 6% -> 0% of each run, Pallas kernels for 0% -> 0%
where the time goes in v1:
time: 102 us; the launch traced here: 101 us
  Pallas kernels  60.3 us (59%)
  local copies, waits for them, and re-layouts  41 us (40%)
    pallas_call x1, Pallas kernels, on_device(): pl.pallas_call(functools.partial(kernel, R, C, chunks), out_shape=jax.Sha...  60.3 us
    unnamed x3, local copies, waits for them, and re-layouts  39.7 us

profile of v1, /device:TPU:0, one launch (start us, length us, event | category | flops | bytes accessed | tf_op | source)
XLA Modules:
  0.0 101.3 jit_solution(13182823187736160138)
XLA Ops:
  0.0 1.4 %copy.7.src_ref = s32[128,1]{1,0:T(8,128)} copy(s32[128,1]{0,1:T(1,128)} %bitcast.3) | data formatting | bytes 1024 | tf_op jit(solution)/shard_map/reshape | solution.py:328
  1.4 19.1 %copy.8.wg_hbm = bf16[2048,3696]{1,0:T(8,128)(2,1)} copy(bf16[2048,3696]{0,1:T(8,128)(2,1)} %param.9) | data formatting | bytes 30277632 | tf_op args[3]
  20.5 19.1 %copy.9.wu_hbm = bf16[2048,3696]{1,0:T(8,128)(2,1)} copy(bf16[2048,3696]{0,1:T(8,128)(2,1)} %param.10) | data formatting | bytes 30277632 | tf_op args[4]
  39.6 60.3 %feed_forward.1 = bf16[16,2048]{1,0:T(8,128)(2,1)} custom-call(bf16[16,2048]{1,0:T(8,128)(2,1)} %tok_ref.1, s32[128,1]{1,0:T(8,128)} %copy.7.src_ref, f32[1,2048]{1,0:T(1,128)} %bitcast.2, bf16[2048,3696]{1,0:T(8,128)(2,1)} %copy.8.wg_hbm, bf16[2048,3696]{1,0:T(8,128)(2,1)} %copy.9.wu_hbm, bf16[3696,2048]{1,0:T(8,128)(2,1)} %wd_hbm.1), custom_call_target="tpu_custom_call" | custom-call | flops 5813305344 | bytes 45416448 | tf_op jit(solution)/shard_map/feed_forward/pallas_call | solution.py:317
  99.9 1.5 %copy.11 = bf16[16,2048]{1,0:T(8,128)(2,1)} copy(bf16[16,2048]{1,0:T(8,128)(2,1)} %feed_forward.1) | data formatting | bytes 131072
